TPU v7x, 32 devices: a whole 2x2x4 slice. The times are simulated.
32 devices in a mesh: grp: 2 (over x), reg: 4 (over y, core), sub: 4 (over z).
Axes of the slice: x: 2, y: 2, z: 4, core: 2. Of those that a mesh axis runs over, the one named last changes fastest.
Arguments:
- ensemble: float32 [128, 256, 512], P(('grp', 'reg'), None, 'sub'), parts along dimension 0, may hold values from -6 to 6
- stencil: float32 [9, 256], replicated, may hold values from -2 to 2
- forcing: float32 [256, 512], P(None, 'sub'), may hold values from -6 to 6
- obs_lat: int32 [1024], P('grp'), parts along dimension 0, may hold values from 0 to 255
- obs_lon: int32 [1024], P('grp'), parts along dimension 0, may hold values from 0 to 511
- obs_value: float32 [1024], P('grp'), parts along dimension 0, may hold values from -6 to 6
- obs_var: float32 [1024], P('grp'), parts along dimension 0, may hold values from 0.25 to 4
- obs_order: int32 [1024], P('grp'), parts along dimension 0, may hold values from 0 to 511, each once
Outputs:
- analysis: float32 [128, 256, 512], P('grp', 'reg', 'sub'), parts along dimension 0
There are 2 independent parts, one for each index of `grp`. A program takes and returns all parts, laid end to end along the dimension named above; an argument that names none is the same for every part. Nothing has to cross between parts.
Inputs may be any that keep to these rules, and one draw needn't show every extreme that they name: `obs_order`: each of 0 to 511 appears once.
All inputs are finite; a program needn't handle non-finite values.
Results may differ from a plain program's by a relative error of at most 0.0003.
Values sent between devices are 32-bit elements; how exact they have to be, the bound alone decides.
A program may use at most 128 MiB of HBM per device.

v0:
```python
import jax
import jax.numpy as jnp
from jax import lax
from jax.sharding import PartitionSpec as P

BATCH = 256
NBATCH = 2


small_jitter = 1e-06


def padded_2(value, sides, width):
    for axis, dim in sides:
        size, length = (lax.axis_size(axis), value.shape[dim])
        up = [(i, (i + 1) % size) for i in range(size)]
        down = [(j, i) for i, j in up]
        last = lax.slice_in_dim(value, length - width, length, axis=dim)
        leading = lax.slice_in_dim(value, 0, width, axis=dim)
        before = lax.ppermute(last, axis, up)
        after = lax.ppermute(leading, axis, down)
        value = jnp.concatenate([before, value, after], axis=dim)
    return value


def gaspari_cohn(radius):
    square = radius * radius
    cube = square * radius
    fourth = cube * radius
    fifth = fourth * radius
    inner = -0.25 * fifth + 0.5 * fourth + 0.625 * cube - 5.0 / 3.0 * square + 1.0
    safe = jnp.maximum(radius, 1.0)
    outer = (
        fifth / 12.0
        - 0.5 * fourth
        + 0.625 * cube
        + 5.0 / 3.0 * square
        - 5.0 * radius
        + 4.0
        - 2.0 / 3.0 / safe
    )
    return jnp.where(radius <= 1.0, inner, jnp.where(radius < 2.0, outer, 0.0))


def localize(obs_rows, obs_cols, grid_rows, grid_cols, nlon, half_lat, half_lon):
    lat_gap = jnp.abs(obs_rows[:, None] - grid_rows[None, :]).astype(jnp.float32) / half_lat
    lon_apart = jnp.abs(obs_cols[:, None] - grid_cols[None, :])
    lon_gap = jnp.minimum(lon_apart, nlon - lon_apart).astype(jnp.float32) / half_lon
    radius = jnp.sqrt(
        lat_gap[:, :, None] * lat_gap[:, :, None] + lon_gap[:, None, :] * lon_gap[:, None, :]
    )
    return gaspari_cohn(radius).reshape(obs_rows.shape[0], -1)


def obs_update(prior, values, variances, members):
    prior_mean = jnp.mean(prior, axis=0)
    anomaly = prior - prior_mean
    spread = jnp.sum(anomaly * anomaly, axis=0) / (members - 1.0)
    combined = spread + variances
    post_mean = (prior_mean * variances + values * spread) / combined
    shrink = jnp.sqrt(variances / combined)
    shift_obs = post_mean - prior_mean + (shrink - 1.0) * anomaly
    return (anomaly, spread, shift_obs)


def regress(block, anomaly, spread, shift_obs, locality):
    members = block.shape[0]
    covar = jnp.dot(
        anomaly.T, block, precision=lax.Precision.HIGHEST, preferred_element_type=jnp.float32
    ) / (members - 1.0)
    gain = covar * locality / (spread + small_jitter)[:, None]
    return block + jnp.dot(
        shift_obs, gain, precision=lax.Precision.HIGHEST, preferred_element_type=jnp.float32
    )


def learned_advance(padded, weights, forcing_part):
    rows_out = padded.shape[1] - 2
    cols_out = padded.shape[2] - 2
    tendency = forcing_part[None, :, :]
    for row_shift in range(3):
        for col_shift in range(3):
            tendency = (
                tendency
                + weights[3 * row_shift + col_shift][None, :, None]
                * padded[:, row_shift : row_shift + rows_out, col_shift : col_shift + cols_out]
            )
    return padded[:, 1:-1, 1:-1] + jnp.tanh(tendency)


def per_device(ensemble, stencil, forcing, obs_lat, obs_lon, obs_value, obs_var, obs_order):
    reg_count = lax.axis_size("reg")
    subgroup_count = lax.axis_size("sub")
    reg_index = lax.axis_index("reg")
    sub_index = lax.axis_index("sub")
    nlat = stencil.shape[1]
    lat_dev = nlat // reg_count
    lon_dev = ensemble.shape[2]
    nlon = lon_dev * subgroup_count
    half_lat = nlat // 3
    half_lon = nlon // 8
    widened_slab = padded_2(ensemble, (("sub", 2),), 1)
    widened_slab = jnp.pad(widened_slab, ((0, 0), (1, 1), (0, 0)))
    predicted_state = learned_advance(widened_slab, stencil, forcing)
    present_state = lax.all_to_all(predicted_state, "reg", split_axis=1, concat_axis=0, tiled=True)
    members = present_state.shape[0]
    flat_state = present_state.reshape(members, lat_dev * lon_dev)
    grid_rows = reg_index * lat_dev + jnp.arange(lat_dev, dtype=jnp.int32)
    grid_cols = sub_index * lon_dev + jnp.arange(lon_dev, dtype=jnp.int32)
    for batch_index in range(NBATCH):
        chosen = obs_order[batch_index * BATCH : (batch_index + 1) * BATCH]
        obs_rows = jnp.take(obs_lat, chosen)
        obs_cols = jnp.take(obs_lon, chosen)
        owned = (obs_rows // lat_dev == reg_index) & (obs_cols // lon_dev == sub_index)
        local_cell = jnp.clip(
            (obs_rows - reg_index * lat_dev) * lon_dev + (obs_cols - sub_index * lon_dev),
            0,
            lat_dev * lon_dev - 1,
        )
        local_priors = jnp.where(owned[None, :], jnp.take(flat_state, local_cell, axis=1), 0.0)
        prior = lax.psum(local_priors, ("reg", "sub"))
        anomaly, spread, shift_obs = obs_update(
            prior, jnp.take(obs_value, chosen), jnp.take(obs_var, chosen), members
        )
        locality = localize(obs_rows, obs_cols, grid_rows, grid_cols, nlon, half_lat, half_lon)
        flat_state = regress(flat_state, anomaly, spread, shift_obs, locality)
    return flat_state.reshape(members, lat_dev, lon_dev)


def solution(mesh):
    return jax.shard_map(
        per_device,
        mesh=mesh,
        in_specs=(
            P(("grp", "reg"), None, "sub"),
            P(),
            P(None, "sub"),
            P("grp"),
            P("grp"),
            P("grp"),
            P("grp"),
            P("grp"),
        ),
        out_specs=P("grp", "reg", "sub"),
        check_vma=False,
    )
```

profile of v0, /device:TPU:0, one launch (start us, length us, event | category | flops | bytes accessed | tf_op | source)
XLA Modules:
  0.0 337.3 jit_solution(10912383714616016098)
XLA Ops:
  6.5 4.3 %fusion.67 = (f32[16,256,1]{2,1,0:T(8,128)}, f32[16,256,1]{2,1,0:T(8,128)S(1)}) fusion(f32[16,256,128]{2,1,0:T(8,128)} %param.14), kind=kLoop, calls=%fused_computation.160 | loop fusion | bytes 65536 | tf_op jit(solution)/shard_map/slice | solution.py:18
  10.8 2.2 copy.45
  13.0 3.0 collective-permute-start
  16.1 0.6 copy.46
  16.7 2.1 collective-permute-start.1
  18.8 1.9 gather_fusion
  20.7 1.9 gather_fusion.1
  22.7 1.9 gather_fusion.5
  24.6 1.9 gather_fusion.6
  26.7 2.8 copy.39
  29.5 2.4 copy.31
  31.9 2.4 copy.33
  34.3 4.2 %select_maximum_fusion = f32[16,258,130]{2,0,1:T(8,128)S(1)} fusion(f32[16,256,1]{2,0,1:T(8,128)} %copy.33, f32[16,256,128]{2,0,1:T(8,128)S(1)} %copy.39, f32[16,256,1]{2,0,1:T(8,128)} %copy.31), kind=kLoop, calls=%fused_computation.54 | loop fusion | flops 4293120 | bytes 4276480 | tf_op jit(solution)/shard_map/concatenate | solution.py:22
  38.5 7.8 %fusion.27 = f32[16,256,128]{2,0,1:T(8,128)} fusion(f32[16,256,128]{2,0,1:T(8,128)S(1)} %copy.39, f32[16,258,130]{2,0,1:T(8,128)S(1)} %select_maximum_fusion, f32[16,256,1]{2,0,1:T(8,128)S(1)} %copy-done.6, f32[16,256,1]{2,0,1:T(8,128)S(1)} %copy-done.5, f32[256]{0:T(256)S(1)} %bitcast.119, f32[256]{0:T(256)S(1)} %bitcast.120, f32[256]{0:T(256)S(1)} %bitcast.113, ...), kind=kLoop, calls=%fused_computation.61 | loop fusion | flops 11010048 | bytes 16950272 | tf_op jit(solution)/shard_map/add | solution.py:88
  46.2 3.6 %all-to-all-start = ((f32[16,256,128]{2,0,1:T(8,128)}), f32[16,256,128]{2,0,1:T(8,128)S(1)}, u32[]{:S(2)}, u32[]{:S(2)}) async-start(f32[16,256,128]{2,0,1:T(8,128)} %fusion.27), calls=%async_computation | async-start | bytes 4194304 | tf_op jit(solution)/shard_map/all_to_all | solution.py:105
  49.9 0.0 all-reduce.4.cloned.1.call-start
  49.9 0.1 multiply_multiply_fusion.4
  50.0 0.1 copy.42
  50.2 0.2 fusion.44
  50.3 4.6 %add_sqrt_fusion.1 = f32[256,64,128]{2,1,0:T(8,128)} fusion(f32[256,128]{1,0:T(8,128)S(1)} %get-tuple-element.43, f32[256,64]{1,0:T(8,128)S(1)} %copy.42), kind=kLoop, calls=%fused_computation.51 | loop fusion | flops 2097152 | bytes 8585216 | tf_op jit(solution)/shard_map/sqrt | solution.py:49
  54.9 20.6 %all-to-all-done = f32[16,256,128]{2,0,1:T(8,128)S(1)} async-done(((f32[16,256,128]{2,0,1:T(8,128)}), f32[16,256,128]{2,0,1:T(8,128)S(1)}, u32[]{:S(2)}, u32[]{:S(2)}) %all-to-all-start) | async-done | bytes 2097184 | tf_op jit(solution)/shard_map/all_to_all | solution.py:105
  75.5 1.3 copy-done.8
  76.8 2.2 copy.40
  79.1 2.5 copy.57
  81.6 3.8 %copy.41 = f32[64,8192]{0,1:T(8,128)} copy(f32[64,8192]{1,0:T(8,128)} %bitcast.108) | data formatting | bytes 4194304 | tf_op jit(solution)/shard_map/reshape | solution.py:107
  85.4 2.9 gather_fusion.2
  88.3 0.8 bitcast_select_fusion.1
  89.1 0.2 all-reduce.6.cloned.1.call-start
  89.4 1.9 gather_fusion.3
  91.4 1.9 gather_fusion.4
  93.3 0.1 copy.44
  93.4 81.5 %all-reduce.4.cloned.1.call-done = f32[64,256]{0,1:T(8,128)} async-done(((f32[64,256]{0,1:T(8,128)}), f32[64,256]{0,1:T(8,128)}) %all-reduce.4.cloned.1.call-update) | async-done | bytes 65552 | tf_op jit(solution)/shard_map/psum | solution.py:121
  174.9 1.0 reduce_sum.36
  175.9 1.1 multiply_reduce_fusion.1
  177.0 22.5 %fusion.10 = f32[256,8192]{1,0:T(8,128)S(1)} fusion(f32[32,8,64,128]{3,2,1,0:T(8,128)} %bitcast.109, f32[256]{0:T(256)S(1)} %get-tuple-element.39, f32[64,256]{0,1:T(8,128)} %all-reduce.4.cloned.1.call-done, f32[256]{0:T(256)S(1)} %broadcast_multiply_fusion.1, f32[8,8,64,128]{3,2,1,0:T(8,128)S(1)} %bitcast.106), kind=kOutput, calls=%fused_computation.28 | convolution fusion | flops 1671446528 | bytes 18941952 | tf_op jit(solution)/shard_map/dot_general | solution.py:68
  199.5 7.8 %convolution_add_fusion.1 = f32[64,8192]{1,0:T(8,128)S(1)} fusion(f32[256,8192]{1,0:T(8,128)S(1)} %fusion.10, f32[64,256]{0,1:T(8,128)S(1)} %copy-done.9, f32[256]{0:T(256)S(1)} %get-tuple-element.32, f32[256]{0:T(256)S(1)} %get-tuple-element.31, f32[256]{0:T(256)S(1)} %broadcast_multiply_fusion.1, f32[8,8,64,128]{3,2,1,0:T(8,128)} %bitcast.107), kind=kOutput, calls=%fused_computation.27 | convolution fusion | flops 1611186176 | bytes 12651520 | tf_op jit(solution)/shard_map/dot_general | solution.py:72
  207.3 2.7 copy.43
  210.0 2.9 gather_fusion.7
  212.9 0.8 bitcast_select_fusion
  213.7 4.6 %add_sqrt_fusion = f32[256,64,128]{2,1,0:T(8,128)} fusion(f32[256,128]{1,0:T(8,128)S(1)} %get-tuple-element.42, f32[256,64]{1,0:T(8,128)S(1)} %copy.44), kind=kLoop, calls=%fused_computation.50 | loop fusion | flops 2097152 | bytes 8585216 | tf_op jit(solution)/shard_map/sqrt | solution.py:49
  218.3 1.9 gather_fusion.8
  220.3 1.9 gather_fusion.9
  222.2 80.2 %all-reduce.6.cloned.1.call-done = f32[64,256]{0,1:T(8,128)} async-done(((f32[64,256]{0,1:T(8,128)}), f32[64,256]{0,1:T(8,128)}) %all-reduce.6.cloned.1.call-update) | async-done | bytes 65552 | tf_op jit(solution)/shard_map/psum | solution.py:121
  302.4 1.0 reduce_sum.38
  303.5 1.1 multiply_reduce_fusion
  304.6 18.9 %fusion.11 = f32[256,8192]{1,0:T(8,128)S(1)} fusion(f32[64,8192]{1,0:T(8,128)S(1)} %convolution_add_fusion.1, f32[32,8,64,128]{3,2,1,0:T(8,128)} %bitcast.110, f32[256]{0:T(256)S(1)} %get-tuple-element.38, f32[64,256]{0,1:T(8,128)} %all-reduce.6.cloned.1.call-done, f32[256]{0:T(256)S(1)} %broadcast_multiply_fusion), kind=kOutput, calls=%fused_computation.29 | convolution fusion | flops 1671446528 | bytes 18941952 | tf_op jit(solution)/shard_map/dot_general | solution.py:68
  323.5 5.3 %fusion.38 = f32[8,8,64,128]{3,1,2,0:T(8,128)S(1)} fusion(f32[64,8192]{1,0:T(8,128)S(1)} %convolution_add_fusion.1, f32[256,8192]{1,0:T(8,128)S(1)} %fusion.11, f32[64,256]{0,1:T(8,128)S(1)} %copy-done.10, f32[256]{0:T(256)S(1)} %get-tuple-element.30, f32[256]{0:T(256)S(1)} %get-tuple-element.29, f32[256]{0:T(256)S(1)} %broadcast_multiply_fusion), kind=kOutput, calls=%fused_computation.79 | convolution fusion | flops 1611186176 | bytes 12651520 | tf_op jit(solution)/shard_map/dot_general | solution.py:72
  328.8 1.7 copy.50
  (45 shorter events, 0.2 us)
Async XLA Ops:
  6.5 12.2 %copy-start = (s32[512]{0:T(512)S(1)}, s32[512]{0:T(512)}, u32[]{:S(2)}) copy-start(s32[512]{0:T(512)} %param.17) | copy-start | bytes 6148
  6.5 12.2 %copy-start.12 = (s32[512]{0:T(512)S(1)}, s32[512]{0:T(512)}, u32[]{:S(2)}) copy-start(s32[512]{0:T(512)} %param.21) | copy-start | bytes 6148
  6.5 14.2 %copy-start.2 = (s32[512]{0:T(512)S(1)}, s32[512]{0:T(512)}, u32[]{:S(2)}) copy-start(s32[512]{0:T(512)} %param.18) | copy-start | bytes 6148
  6.5 20.1 %copy-start.13 = (f32[9,256]{1,0:T(8,128)S(1)}, f32[9,256]{1,0:T(8,128)}, u32[]{:S(2)}) copy-start(f32[9,256]{1,0:T(8,128)} %param.15) | copy-start | bytes 27652
  13.0 16.5 %collective-permute-start = (f32[16,256,1]{1,0,2:T(8,128)S(1)}, f32[16,256,1]{1,0,2:T(8,128)S(1)}, u32[]{:S(2)}, u32[]{:S(2)}) collective-permute-start(f32[16,256,1]{1,0,2:T(8,128)S(1)} %copy.45), channel_id=1, source_target_pairs={{0,1},{1,2},{2,3},{3,0},{4,5},{5,6},{6,7},{7,4},{8,9},{9,10},{10,1... | collective-permute-start | bytes 49160 | tf_op jit(solution)/shard_map/ppermute | solution.py:20
  16.7 15.2 %collective-permute-start.1 = (f32[16,256,1]{1,0,2:T(8,128)S(1)}, f32[16,256,1]{1,0,2:T(8,128)S(1)}, u32[]{:S(2)}, u32[]{:S(2)}) collective-permute-start(f32[16,256,1]{1,0,2:T(8,128)S(1)} %copy.46), channel_id=1, source_target_pairs={{1,0},{2,1},{3,2},{0,3},{5,4},{6,5},{7,6},{4,7},{9,8},{10,9},{11,1... | collective-permute-start | bytes 49160 | tf_op jit(solution)/shard_map/ppermute | solution.py:21
  29.5 9.0 %copy-start.11 = (f32[256,128]{1,0:T(8,128)S(1)}, f32[256,128]{1,0:T(8,128)}, u32[]{:S(2)}) copy-start(f32[256,128]{1,0:T(8,128)} %param.16) | copy-start | bytes 393220
  34.3 4.2 %copy-start.5 = (f32[16,256,1]{2,0,1:T(8,128)S(1)}, f32[16,256,1]{2,0,1:T(8,128)}, u32[]{:S(2)}) copy-start(f32[16,256,1]{2,0,1:T(8,128)} %copy.31) | copy-start | bytes 49156
  34.3 4.2 %copy-start.6 = (f32[16,256,1]{2,0,1:T(8,128)S(1)}, f32[16,256,1]{2,0,1:T(8,128)}, u32[]{:S(2)}) copy-start(f32[16,256,1]{2,0,1:T(8,128)} %copy.33) | copy-start | bytes 49156
  46.2 29.3 %all-to-all-start = ((f32[16,256,128]{2,0,1:T(8,128)}), f32[16,256,128]{2,0,1:T(8,128)S(1)}, u32[]{:S(2)}, u32[]{:S(2)}) async-start(f32[16,256,128]{2,0,1:T(8,128)} %fusion.27), calls=%async_computation | async-start | bytes 4194304 | tf_op jit(solution)/shard_map/all_to_all | solution.py:105
  49.9 125.0 %all-reduce.4.cloned.1.call-start = ((), (), s32[]{:S(2)}) async-start(), calls=%async_computation.1 | async-start | bytes 262144 | tf_op jit(solution)/shard_map/psum | solution.py:121
  54.9 34.5 %copy-start.3 = (f32[512]{0:T(512)S(1)}, f32[512]{0:T(512)}, u32[]{:S(2)}) copy-start(f32[512]{0:T(512)} %param.20) | copy-start | bytes 6148
  54.9 36.4 %copy-start.4 = (f32[512]{0:T(512)S(1)}, f32[512]{0:T(512)}, u32[]{:S(2)}) copy-start(f32[512]{0:T(512)} %param.19) | copy-start | bytes 6148
  75.5 1.3 copy-start.8
  79.1 120.4 %copy-start.7 = (f32[16,4,64,128]{3,2,0,1:T(8,128)}, f32[16,4,64,128]{3,2,0,1:T(8,128)S(1)}, u32[]{:S(2)}) copy-start(f32[16,4,64,128]{3,2,0,1:T(8,128)S(1)} %copy.40) | copy-start | bytes 6291460
  89.1 213.3 %all-reduce.6.cloned.1.call-start = ((), (), s32[]{:S(2)}) async-start(), calls=%async_computation.2 | async-start | bytes 262144 | tf_op jit(solution)/shard_map/psum | solution.py:121
  177.0 22.5 %copy-start.9 = (f32[64,256]{0,1:T(8,128)S(1)}, f32[64,256]{0,1:T(8,128)}, u32[]{:S(2)}) copy-start(f32[64,256]{0,1:T(8,128)} %all-reduce.4.cloned.1.call-done) | copy-start | bytes 196612
  304.6 18.9 %copy-start.10 = (f32[64,256]{0,1:T(8,128)S(1)}, f32[64,256]{0,1:T(8,128)}, u32[]{:S(2)}) copy-start(f32[64,256]{0,1:T(8,128)} %all-reduce.6.cloned.1.call-done) | copy-start | bytes 196612
  323.4 7.1 %copy-start.1 = (s32[512]{0:T(512)S(1)}, s32[512]{0:T(512)}, u32[]{:S(2)}) copy-start(s32[512]{0:T(512)} %param.17) | copy-start | bytes 6148
Sparse Core Ops, SparseCore 0:
  89.3 85.5 all-reduce.3
  213.9 88.5 all-reduce.5
where the time goes:
time: 339 us; the launch traced here: 337 us
  waiting for transfers between devices  182 us (54%)
  matrix products  54.4 us (16%)
  local copies, waits for them, and re-layouts  50.6 us (15%)
  other arithmetic  27.2 us (8%)
  between operations  13.8 us (4%)
  starting transfers between devices  8.98 us (3%)
    psum x2, waiting for transfers between devices, per_device(): prior = lax.psum(local_priors, ('reg', 'sub'))  162 us
    dot_general x2, matrix products, regress(): jnp.dot(anomaly.T, block, precision=lax.Precision.HIGHEST, preferred_elem...  41.3 us
    all_to_all x1, waiting for transfers between devices, per_device(): lax.all_to_all(predicted_state, 'reg', split_axis=1, concat_axis=0, tiled...  20.6 us
    dot_general x2, matrix products, regress(): jnp.dot(shift_obs, gain, precision=lax.Precision.HIGHEST, preferred_eleme...  13.1 us
    unnamed x33, local copies, waits for them, and re-layouts  11.2 us
    sqrt x2, other arithmetic, localize(): jnp.sqrt(lat_gap[:, :, None] * lat_gap[:, :, None] + lon_gap[:, None, :]...  9.14 us
    add x1, other arithmetic, learned_advance(): return padded[:, 1:-1, 1:-1] + jnp.tanh(tendency)  7.77 us
  transfers between devices with their start and end apart: 5, of which 3 were waited for; matrix products, arithmetic and copies ran while one was open for 9% of the time, Pallas kernels for 0%

commit v1 on v0

v1 whole, which is shorter than its diff:
```python
import functools

import jax
import jax.numpy as jnp
from jax import lax
from jax.experimental import pallas as pl
from jax.experimental.pallas import tpu as pltpu
from jax.sharding import PartitionSpec as P

BATCH = 256
NBATCH = 2
CH = 8
LANES = 128
small_jitter = 1e-06
MESH = pl.DeviceIdType.MESH


def locality_of(u):
    u = jnp.minimum(u, 4.0)
    r = lax.rsqrt(jnp.maximum(u, 1e-12))
    q = u * r
    s = 0.5 * u - 5.0 / 3.0
    us = u * s
    inner = 1.0 + us + (u * q) * (0.625 - 0.25 * u)
    outer = 4.0 - us + q * (u * (0.625 + u * (1.0 / 12.0)) - 5.0) - (2.0 / 3.0) * r
    return jnp.where(u <= 1.0, inner, jnp.where(u < 4.0, outer, 0.0))


def split(value):
    hi = value.astype(jnp.bfloat16)
    lo = (value - hi.astype(jnp.float32)).astype(jnp.bfloat16)
    return hi, lo


def apply_update(x, lhs, shifts, locality):
    members = x.shape[0]
    hi, lo = split(x)
    rhs = jnp.concatenate([hi, lo, hi, lo], axis=0)
    gain = jnp.dot(lhs, rhs, preferred_element_type=jnp.float32) * locality
    g_hi, g_lo = split(gain)
    both = jnp.dot(shifts, g_hi, preferred_element_type=jnp.float32)
    rest = jnp.dot(shifts[:members], g_lo, preferred_element_type=jnp.float32)
    return x + both[:members] + both[members:] + rest


def kernel(
    dims, ens_ref, sten_ref, forc_ref, lat_ref, lon_ref, val_ref, var_ref, ord_ref, out_ref,
    ep, fc, xs, loc, wt, wb, hsend, hrecv, hp, edge_l, edge_r, obs, pall, p_sub, p_reg, lhs_s, shift_s, xw,
    ens_sem, h_ssem, h_rsem, b_ssem, b_rsem, ps_ssem, ps_rsem, pr_ssem, pr_rsem,
):
    reg_count, sub_count, mem, nlat, nlon, lat_dev, side, nobs = dims
    f32 = jnp.float32
    members = mem * reg_count
    nq = lat_dev // CH
    half = nq // 2
    me = lax.axis_index("reg")
    my_sub = lax.axis_index("sub")
    right = lax.rem(my_sub + 1, sub_count)
    left = lax.rem(my_sub + sub_count - 1, sub_count)

    load = pltpu.make_async_copy(ens_ref, ep.at[:, pl.ds(8, nlat), :], ens_sem)
    load.start()
    hrecv[...] = jnp.zeros_like(hrecv)

    barrier = pltpu.get_barrier_semaphore()
    for d in range(1, reg_count):
        pl.semaphore_signal(barrier, inc=1, device_id={"reg": lax.rem(me + d, reg_count)}, device_id_type=MESH)
    for d in range(1, sub_count):
        pl.semaphore_signal(barrier, inc=1, device_id={"sub": lax.rem(my_sub + d, sub_count)}, device_id_type=MESH)

    ep[:, 0:8, :] = jnp.zeros((mem, 8, LANES), f32)
    ep[:, nlat + 8 : nlat + 16, :] = jnp.zeros((mem, 8, LANES), f32)
    hp[0:8, :] = jnp.zeros((8, LANES), f32)
    hp[nlat + 8 : nlat + 16, :] = jnp.zeros((8, LANES), f32)
    lane = lax.broadcasted_iota(jnp.int32, (nlat, LANES), 1)
    load.wait()
    packed = jnp.zeros((nlat, LANES), f32)
    for m in range(mem):
        packed = jnp.where(lane == m, ep[m, 8 : nlat + 8, 0:1], packed)
        packed = jnp.where(lane == side + m, ep[m, 8 : nlat + 8, LANES - 1 : LANES], packed)
    hsend[...] = jnp.transpose(packed)[0 : 2 * side]
    pl.semaphore_wait(barrier, reg_count + sub_count - 2)

    to_left = pltpu.make_async_remote_copy(
        src_ref=hsend.at[pl.ds(0, side)], dst_ref=hrecv.at[pl.ds(side, side)],
        send_sem=h_ssem.at[0], recv_sem=h_rsem.at[1], device_id={"sub": left}, device_id_type=MESH)
    to_right = pltpu.make_async_remote_copy(
        src_ref=hsend.at[pl.ds(side, side)], dst_ref=hrecv.at[pl.ds(0, side)],
        send_sem=h_ssem.at[1], recv_sem=h_rsem.at[0], device_id={"sub": right}, device_id_type=MESH)
    to_left.start()
    to_right.start()

    obs[...] = jnp.zeros_like(obs)
    obs[0:1, :] = lat_ref[...].astype(f32)
    obs[1:2, :] = lon_ref[...].astype(f32)
    obs[2:3, :] = val_ref[...]
    obs[3:4, :] = var_ref[...]
    columns = jnp.transpose(obs[...])
    picked = lax.broadcasted_iota(jnp.int32, (nobs, nobs), 0) == ord_ref[...]
    for i in range(4):
        obs[i : i + 1, :] = jnp.sum(jnp.where(picked, columns[:, i : i + 1], 0.0), axis=0, keepdims=True)
    ordered = jnp.transpose(obs[...])
    lat_col = [ordered[b * BATCH : (b + 1) * BATCH, 0:1] for b in range(NBATCH)]
    lon_col = [ordered[b * BATCH : (b + 1) * BATCH, 1:2] for b in range(NBATCH)]
    scale_lat = 1.0 / (nlat // 3)
    scale_lon = 1.0 / (nlon // 8)
    lat_row = obs[0:1, :]
    lon_row = obs[1:2, :]

    wt[...] = jnp.zeros_like(wt)
    wt[0:9, :] = sten_ref[...]
    taps = jnp.transpose(wt[...])
    for t in range(9):
        wb[t] = jnp.broadcast_to(taps[:, t : t + 1], (nlat, LANES))

    to_left.wait()
    to_right.wait()
    hp[8 : nlat + 8, :] = jnp.transpose(hrecv[...])
    h_prev, h_cur, h_next = hp[7 : nlat + 7, :], hp[8 : nlat + 8, :], hp[9 : nlat + 9, :]
    edge_l[...] = wb[0] * h_prev + wb[3] * h_cur + wb[6] * h_next
    edge_r[...] = wb[2] * h_prev + wb[5] * h_cur + wb[8] * h_next

    small_lane = lax.broadcasted_iota(jnp.int32, (CH, LANES), 1)

    def forecast(q, d):
        target = lax.rem(me + d, reg_count)
        base = pl.multiple_of(target * lat_dev + q * CH, CH)
        rows = pl.ds(base, CH)
        block = ep[:, pl.ds(base, 3 * CH), :]
        before, now, after = block[:, CH - 1 : 2 * CH - 1], block[:, CH : 2 * CH], block[:, CH + 1 : 2 * CH + 1]

        def tapped(j):
            return wb[j, rows, :] * before + wb[3 + j, rows, :] * now + wb[6 + j, rows, :] * after

        from_left = pltpu.roll(tapped(0).reshape(mem * CH, LANES), 1, 1).reshape(mem, CH, LANES)
        from_right = pltpu.roll(tapped(2).reshape(mem * CH, LANES), LANES - 1, 1).reshape(mem, CH, LANES)
        middle = tapped(1) + forc_ref[rows, :]
        el, er = edge_l[rows, :], edge_r[rows, :]
        for m in range(mem):
            a = jnp.where(small_lane == 0, el[:, m : m + 1], from_left[m])
            b = jnp.where(small_lane == LANES - 1, er[:, side + m : side + m + 1], from_right[m])
            fc[m, rows, :] = now[m] + jnp.tanh(middle[m] + a + b)

    def band_copy(q, d):
        target = lax.rem(me + d, reg_count)
        base = pl.multiple_of(target * lat_dev + q * CH, CH)
        return pltpu.make_async_remote_copy(
            src_ref=fc.at[:, pl.ds(base, CH), :],
            dst_ref=xs.at[pl.ds(me * mem, mem), pl.ds(pl.multiple_of(q * CH, CH), CH), :],
            send_sem=b_ssem.at[q, target], recv_sem=b_rsem.at[q, me],
            device_id={"reg": target}, device_id_type=MESH)

    def band_arrival(q, d):
        source = lax.rem(me + d, reg_count)
        base = pl.multiple_of(source * lat_dev + q * CH, CH)
        return pltpu.make_async_remote_copy(
            src_ref=fc.at[:, pl.ds(base, CH), :],
            dst_ref=xs.at[pl.ds(source * mem, mem), pl.ds(pl.multiple_of(q * CH, CH), CH), :],
            send_sem=b_ssem.at[q, source], recv_sem=b_rsem.at[q, source],
            device_id={"reg": source}, device_id_type=MESH)

    @pl.loop(0, half)
    def _(q):
        @pl.loop(1, reg_count)
        def _(d):
            forecast(q, d)
            band_copy(q, d).start()

    @pl.loop(half, nq)
    def _(q):
        @pl.loop(1, reg_count)
        def _(d):
            forecast(q, d)

    @pl.loop(0, nq)
    def _(q):
        forecast(q, 0)

    first_col = (my_sub * LANES).astype(f32)
    here = (lax.broadcasted_iota(jnp.int32, (LANES, nobs), 0).astype(f32) + first_col) == lon_row
    here = jnp.where(here, 1.0, 0.0).astype(jnp.bfloat16)
    here = jnp.concatenate([here, here], axis=0)
    on_row = lax.broadcasted_iota(jnp.int32, (nlat, nobs), 0).astype(f32) == lat_row
    p_sub[0] = jnp.zeros_like(p_sub[0])

    @pl.loop(0, mem)
    def _(m):
        hi, lo = split(fc[m])
        found = jnp.dot(jnp.concatenate([hi, lo], axis=1), here, preferred_element_type=f32)
        p_sub[0, pl.ds(m, 1), :] = jnp.sum(jnp.where(on_row, found, 0.0), axis=0, keepdims=True)

    sub_copies = []
    for d in range(1, sub_count):
        sub_copies.append(pltpu.make_async_remote_copy(
            src_ref=p_sub.at[0], dst_ref=p_sub.at[d], send_sem=ps_ssem.at[d], recv_sem=ps_rsem.at[d],
            device_id={"sub": lax.rem(my_sub + d, sub_count)}, device_id_type=MESH))
        sub_copies[-1].start()

    own = pl.multiple_of(me * lat_dev, CH)
    xs[pl.ds(me * mem, mem), :, :] = fc[:, pl.ds(own, lat_dev), :]

    first_row = (me * lat_dev).astype(f32)
    lon_here = lax.broadcasted_iota(jnp.int32, (BATCH, LANES), 1).astype(f32) + first_col

    def lon_part(columns_a, columns_b):
        apart = jnp.abs(columns_a - columns_b)
        gap = jnp.minimum(apart, nlon - apart) * scale_lon
        return gap * gap

    def fill_locality(b, low, high):
        lon_sq = lon_part(lon_col[b], lon_here)
        lat_of = lat_col[b] - first_row

        @pl.loop(low, high)
        def _(r):
            gap = (lat_of - r.astype(f32)) * scale_lat
            loc[b, r] = locality_of(gap * gap + lon_sq)

    for copy in sub_copies:
        copy.wait()
    total = p_sub[0]
    for d in range(1, sub_count):
        total = total + p_sub[d]
    p_reg[me] = total
    reg_copies = []
    for d in range(1, reg_count):
        target = lax.rem(me + d, reg_count)
        reg_copies.append(pltpu.make_async_remote_copy(
            src_ref=p_reg.at[me], dst_ref=p_reg.at[me], send_sem=pr_ssem.at[target], recv_sem=pr_rsem.at[me],
            device_id={"reg": target}, device_id_type=MESH))
        reg_copies[-1].start()

    @pl.loop(half, nq)
    def _(q):
        @pl.loop(1, reg_count)
        def _(d):
            band_copy(q, d).start()

    for b in range(NBATCH):
        fill_locality(b, 0, lat_dev)

    for d in range(1, reg_count):
        source = lax.rem(me + d, reg_count)
        pltpu.make_async_remote_copy(
            src_ref=p_reg.at[source], dst_ref=p_reg.at[source], send_sem=pr_ssem.at[source],
            recv_sem=pr_rsem.at[source], device_id={"reg": source}, device_id_type=MESH).wait_recv()
    for j in range(reg_count):
        pall[j * mem : (j + 1) * mem, :] = p_reg[j, 0:mem, :]

    prior = pall[:, 0:BATCH]
    for b in range(NBATCH):
        here_b = slice(b * BATCH, (b + 1) * BATCH)
        values, variances = obs[2:3, here_b], obs[3:4, here_b]
        prior_mean = jnp.sum(prior, axis=0, keepdims=True) * (1.0 / members)
        anomaly = prior - prior_mean
        spread = jnp.sum(anomaly * anomaly, axis=0, keepdims=True) * (1.0 / (members - 1.0))
        combined = spread + variances
        post_mean = (prior_mean * variances + values * spread) / combined
        shift = post_mean - prior_mean + (jnp.sqrt(variances / combined) - 1.0) * anomaly
        scaled = anomaly / ((members - 1.0) * (spread + small_jitter))
        hi = scaled.astype(jnp.bfloat16).astype(f32)
        lo = scaled - hi
        lhs_s[b] = jnp.transpose(jnp.concatenate([hi, hi, lo, lo], axis=0)).astype(jnp.bfloat16)
        shift_s[b] = jnp.concatenate(split(shift), axis=0)
        if b + 1 < NBATCH:
            later = slice((b + 1) * BATCH, (b + 2) * BATCH)
            gap = (lat_col[b] - lat_row[:, later]) * scale_lat
            site = locality_of(gap * gap + lon_part(lon_col[b], lon_row[:, later]))
            prior = apply_update(pall[:, later], lhs_s[b], shift_s[b], site)

    @pl.loop(0, nq)
    def _(q):
        @pl.loop(1, reg_count)
        def _(d):
            band_arrival(q, d).wait_recv()

        rows = pl.ds(pl.multiple_of(q * CH, CH), CH)
        chunk = jnp.swapaxes(xs[:, rows, :], 0, 1)
        xw[...] = jnp.concatenate([chunk[i] for i in range(CH)], axis=1)

        @pl.loop(0, NBATCH)
        def _(b):
            locality = jnp.concatenate([loc[b, q * CH + i] for i in range(CH)], axis=1)
            xw[...] = apply_update(xw[...], lhs_s[b], shift_s[b], locality)

        x = xw[...]
        done = jnp.stack([x[:, i * LANES : (i + 1) * LANES] for i in range(CH)], axis=0)
        out_ref[:, rows, :] = jnp.swapaxes(done, 0, 1)

    for copy in reg_copies:
        copy.wait_send()

    @pl.loop(0, nq)
    def _(q):
        @pl.loop(1, reg_count)
        def _(d):
            band_copy(q, d).wait_send()


def per_device(reg_count, sub_count, ensemble, stencil, forcing, obs_lat, obs_lon, obs_value, obs_var, obs_order):
    mem, nlat, lon_dev = ensemble.shape
    nobs = obs_lat.shape[0]
    lat_dev = nlat // reg_count
    members = mem * reg_count
    side = -(-mem // 8) * 8
    nq = lat_dev // CH
    f32, bf16 = jnp.float32, jnp.bfloat16
    dims = (reg_count, sub_count, mem, nlat, lon_dev * sub_count, lat_dev, side, nobs)
    vmem = pl.BlockSpec(memory_space=pltpu.VMEM)
    dma = pltpu.SemaphoreType.DMA
    return pl.pallas_call(
        functools.partial(kernel, dims),
        out_shape=jax.ShapeDtypeStruct((members, lat_dev, lon_dev), f32),
        in_specs=[pl.BlockSpec(memory_space=pl.ANY)] + [vmem] * 7,
        out_specs=vmem,
        scratch_shapes=[
            pltpu.VMEM((mem, nlat + 16, LANES), f32),
            pltpu.VMEM((mem, nlat, LANES), f32),
            pltpu.VMEM((members, lat_dev, LANES), f32),
            pltpu.VMEM((NBATCH, lat_dev, BATCH, LANES), f32),
            pltpu.VMEM((LANES, nlat), f32),
            pltpu.VMEM((9, nlat, LANES), f32),
            pltpu.VMEM((2 * side, nlat), f32),
            pltpu.VMEM((LANES, nlat), f32),
            pltpu.VMEM((nlat + 16, LANES), f32),
            pltpu.VMEM((nlat, LANES), f32),
            pltpu.VMEM((nlat, LANES), f32),
            pltpu.VMEM((LANES, nobs), f32),
            pltpu.VMEM((members, nobs), f32),
            pltpu.VMEM((sub_count, side, nobs), f32),
            pltpu.VMEM((reg_count, side, nobs), f32),
            pltpu.VMEM((NBATCH, BATCH, 4 * members), bf16),
            pltpu.VMEM((NBATCH, 2 * members, BATCH), bf16),
            pltpu.VMEM((members, CH * LANES), f32),
            dma, dma((2,)), dma((2,)), dma((nq, reg_count)), dma((nq, reg_count)),
            dma((sub_count,)), dma((sub_count,)), dma((reg_count,)), dma((reg_count,)),
        ],
        compiler_params=pltpu.CompilerParams(
            collective_id=0, has_side_effects=True, vmem_limit_bytes=52 * 1024 * 1024
        ),
    )(
        ensemble, stencil, forcing, obs_lat.reshape(1, nobs), obs_lon.reshape(1, nobs),
        obs_value.reshape(1, nobs), obs_var.reshape(1, nobs), obs_order.reshape(1, nobs),
    )


def solution(mesh):
    return jax.shard_map(
        functools.partial(per_device, mesh.shape["reg"], mesh.shape["sub"]),
        mesh=mesh,
        in_specs=(
            P(("grp", "reg"), None, "sub"),
            P(),
            P(None, "sub"),
            P("grp"),
            P("grp"),
            P("grp"),
            P("grp"),
            P("grp"),
        ),
        out_specs=P("grp", "reg", "sub"),
        check_vma=False,
    )
```

time: 339 us -> 68.9 us (0.20)
  waiting for transfers between devices: 182 us -> 0 us
  Pallas kernels: 0 us -> 60.4 us
  matrix products: 54.4 us -> 0 us
  local copies, waits for them, and re-layouts: 50.6 us -> 8.19 us
  other arithmetic: 27.2 us -> 0 us
  between operations: 13.8 us -> 0.02 us
  starting transfers between devices: 8.98 us -> 0 us
    psum x2 -> x0, waiting for transfers between devices: 162 us -> none  [per_device(): prior = lax.psum(local_priors, ('reg', 'sub'))]
    pallas_call x0 -> x1, Pallas kernels: none -> 60.4 us  [per_device(): pl.pallas_call(functools.partial(kernel, dims), out_shape=jax.ShapeDtypeS...]
    dot_general x4 -> x0, matrix products: 54.4 us -> none  [the longest x2 41.3 us: regress(): jnp.dot(anomaly.T, block, precision=lax.Precision.HIGHEST, preferred_elem...]
    gather x10 -> x0, local copies, waits for them, and re-layouts: 21.4 us -> none  [the longest x2 5.81 us: per_device(): jnp.take(flat_state, local_cell, axis=1)]
    all_to_all x1 -> x0, waiting for transfers between devices: 20.6 us -> none  [per_device(): lax.all_to_all(predicted_state, 'reg', split_axis=1, concat_axis=0, tiled...]
    sqrt x2 -> x0, other arithmetic: 9.14 us -> none  [localize(): jnp.sqrt(lat_gap[:, :, None] * lat_gap[:, :, None] + lon_gap[:, None, :]...]
    add x3 -> x0, other arithmetic: 7.77 us -> none  [the longest x1 7.77 us: learned_advance(): return padded[:, 1:-1, 1:-1] + jnp.tanh(tendency)]
    ppermute x2 -> x0, starting transfers between devices: 5.11 us -> none  [the longest x1 3.05 us: padded_2(): before = lax.ppermute(last, axis, up)]
  transfers between devices with their start and end apart: 5 -> 0, of which waited for: 3 -> 0; matrix products, arithmetic and copies ran while one was open for 9% -> 0% of each run, Pallas kernels for 0% -> 0%
where the time goes in v1:
time: 68.9 us; the launch traced here: 68.6 us
  Pallas kernels  60.4 us (88%)
  local copies, waits for them, and re-layouts  8.19 us (12%)
    pallas_call x1, Pallas kernels, per_device(): pl.pallas_call(functools.partial(kernel, dims), out_shape=jax.ShapeDtypeS...  60.4 us
    unnamed x15, local copies, waits for them, and re-layouts  8.19 us

profile of v1, /device:TPU:0, one launch (start us, length us, event | category | flops | bytes accessed | tf_op | source)
XLA Modules:
  0.0 68.6 jit_solution(14256233085637624446)
XLA Ops:
  0.0 0.0 copy-start
  0.0 0.9 %copy-done = f32[256,128]{1,0:T(8,128)S(1)} copy-done((f32[256,128]{1,0:T(8,128)S(1)}, f32[256,128]{1,0:T(8,128)}, u32[]{:S(2)}) %copy-start) | copy-done | bytes 131096
  0.9 0.0 copy-start.1
  0.9 0.7 %copy-done.1 = f32[9,256]{1,0:T(8,128)S(1)} copy-done((f32[9,256]{1,0:T(8,128)S(1)}, f32[9,256]{1,0:T(8,128)}, u32[]{:S(2)}) %copy-start.1) | copy-done | bytes 9240
  1.6 0.0 copy-start.2
  1.6 0.7 copy-done.2
  2.3 0.0 copy-start.3
  2.3 0.7 copy-done.3
  3.0 0.0 copy-start.4
  3.0 0.7 copy-done.4
  3.7 0.0 copy-start.5
  3.7 0.7 copy-done.5
  4.4 0.0 copy-start.6
  4.4 0.7 copy-done.6
  5.0 60.4 %shard_map.82 = f32[64,64,128]{2,1,0:T(8,128)} custom-call(f32[16,256,128]{2,1,0:T(8,128)} %ens_ref.1, f32[9,256]{1,0:T(8,128)S(1)} %copy-done.1, f32[256,128]{1,0:T(8,128)S(1)} %copy-done, s32[1,512]{1,0:T(1,128)S(1)} %bitcast.5, s32[1,512]{1,0:T(1,128)S(1)} %bitcast.6, f32[1,512]{1,0:T(1,128)S(1)} %bitcast.7, f32[1,512]{1,0:T(1,128)S(1)} %bitcast.8, ...), custom_call_target="tpu_custom_call" | custom-call | tf_op jit(solution)/shard_map/pallas_call | solution.py:311
  65.4 3.2 %copy.10 = f32[64,64,128]{2,1,0:T(8,128)} copy(f32[64,64,128]{2,1,0:T(8,128)} %shard_map.82) | data formatting | bytes 4194304
Async XLA Ops:
  0.0 0.9 %copy-start = (f32[256,128]{1,0:T(8,128)S(1)}, f32[256,128]{1,0:T(8,128)}, u32[]{:S(2)}) copy-start(f32[256,128]{1,0:T(8,128)} %forc_ref.1) | copy-start | bytes 393220
  0.9 0.7 %copy-start.1 = (f32[9,256]{1,0:T(8,128)S(1)}, f32[9,256]{1,0:T(8,128)}, u32[]{:S(2)}) copy-start(f32[9,256]{1,0:T(8,128)} %sten_ref.1) | copy-start | bytes 27652
  1.6 0.7 copy-start.2
  2.3 0.7 copy-start.3
  3.0 0.7 copy-start.4
  3.7 0.7 copy-start.5
  4.4 0.7 copy-start.6

commit v2 on v1

--- a/solution.py
+++ b/solution.py
@@ -17,13 +17,13 @@
 
 def locality_of(u):
     u = jnp.minimum(u, 4.0)
-    r = lax.rsqrt(jnp.maximum(u, 1e-12))
+    r = lax.rsqrt(u)
     q = u * r
     s = 0.5 * u - 5.0 / 3.0
     us = u * s
     inner = 1.0 + us + (u * q) * (0.625 - 0.25 * u)
     outer = 4.0 - us + q * (u * (0.625 + u * (1.0 / 12.0)) - 5.0) - (2.0 / 3.0) * r
-    return jnp.where(u <= 1.0, inner, jnp.where(u < 4.0, outer, 0.0))
+    return jnp.where(u <= 1.0, inner, outer)
 
 
 def split(value):
@@ -200,12 +200,13 @@
     xs[pl.ds(me * mem, mem), :, :] = fc[:, pl.ds(own, lat_dev), :]
 
     first_row = (me * lat_dev).astype(f32)
+    tiny = 1e-12
     lon_here = lax.broadcasted_iota(jnp.int32, (BATCH, LANES), 1).astype(f32) + first_col
 
     def lon_part(columns_a, columns_b):
         apart = jnp.abs(columns_a - columns_b)
         gap = jnp.minimum(apart, nlon - apart) * scale_lon
-        return gap * gap
+        return gap * gap + tiny
 
     def fill_locality(b, low, high):
         lon_sq = lon_part(lon_col[b], lon_here)
@@ -216,6 +217,8 @@
             gap = (lat_of - r.astype(f32)) * scale_lat
             loc[b, r] = locality_of(gap * gap + lon_sq)
 
+    early = lat_dev // 2
+    fill_locality(0, 0, early)
     for copy in sub_copies:
         copy.wait()
     total = p_sub[0]
@@ -236,7 +239,8 @@
         def _(d):
             band_copy(q, d).start()
 
-    for b in range(NBATCH):
+    fill_locality(0, early, lat_dev)
+    for b in range(1, NBATCH):
         fill_locality(b, 0, lat_dev)
 
     for d in range(1, reg_count):
@@ -311,7 +315,7 @@
     return pl.pallas_call(
         functools.partial(kernel, dims),
         out_shape=jax.ShapeDtypeStruct((members, lat_dev, lon_dev), f32),
-        in_specs=[pl.BlockSpec(memory_space=pl.ANY)] + [vmem] * 7,
+        in_specs=[pl.BlockSpec(memory_space=pltpu.HBM)] + [vmem] * 7,
         out_specs=vmem,
         scratch_shapes=[
             pltpu.VMEM((mem, nlat + 16, LANES), f32),

time: 68.9 us -> 65 us (0.943)
  Pallas kernels: 60.4 us -> 56.4 us
    pallas_call x1, Pallas kernels: 60.4 us -> 56.4 us  [per_device(): pl.pallas_call(functools.partial(kernel, dims), out_shape=jax.ShapeDtypeS...]
where the time goes in v2:
time: 65 us; the launch traced here: 64.6 us
  Pallas kernels  56.4 us (87%)
  local copies, waits for them, and re-layouts  8.19 us (13%)
    pallas_call x1, Pallas kernels, per_device(): pl.pallas_call(functools.partial(kernel, dims), out_shape=jax.ShapeDtypeS...  56.4 us
    unnamed x15, local copies, waits for them, and re-layouts  8.19 us

profile of v2, /device:TPU:0, one launch (start us, length us, event | category | flops | bytes accessed | tf_op | source)
XLA Modules:
  0.0 64.6 jit_solution(6893557873125238117)
XLA Ops:
  0.0 0.0 copy-start
  0.0 0.9 %copy-done = f32[256,128]{1,0:T(8,128)S(1)} copy-done((f32[256,128]{1,0:T(8,128)S(1)}, f32[256,128]{1,0:T(8,128)}, u32[]{:S(2)}) %copy-start) | copy-done | bytes 131096
  0.9 0.0 copy-start.1
  0.9 0.7 %copy-done.1 = f32[9,256]{1,0:T(8,128)S(1)} copy-done((f32[9,256]{1,0:T(8,128)S(1)}, f32[9,256]{1,0:T(8,128)}, u32[]{:S(2)}) %copy-start.1) | copy-done | bytes 9240
  1.6 0.0 copy-start.2
  1.6 0.7 %copy-done.2 = s32[512]{0:T(512)S(1)} copy-done((s32[512]{0:T(512)S(1)}, s32[512]{0:T(512)}, u32[]{:S(2)}) %copy-start.2) | copy-done | bytes 2072
  2.3 0.0 copy-start.3
  2.3 0.7 %copy-done.3 = s32[512]{0:T(512)S(1)} copy-done((s32[512]{0:T(512)S(1)}, s32[512]{0:T(512)}, u32[]{:S(2)}) %copy-start.3) | copy-done | bytes 2072
  3.0 0.0 copy-start.4
  3.0 0.7 %copy-done.4 = f32[512]{0:T(512)S(1)} copy-done((f32[512]{0:T(512)S(1)}, f32[512]{0:T(512)}, u32[]{:S(2)}) %copy-start.4) | copy-done | bytes 2072
  3.7 0.0 copy-start.5
  3.7 0.7 %copy-done.5 = f32[512]{0:T(512)S(1)} copy-done((f32[512]{0:T(512)S(1)}, f32[512]{0:T(512)}, u32[]{:S(2)}) %copy-start.5) | copy-done | bytes 2072
  4.4 0.0 copy-start.6
  4.4 0.7 %copy-done.6 = s32[512]{0:T(512)S(1)} copy-done((s32[512]{0:T(512)S(1)}, s32[512]{0:T(512)}, u32[]{:S(2)}) %copy-start.6) | copy-done | bytes 2072
  5.0 56.4 %shard_map.82 = f32[64,64,128]{2,1,0:T(8,128)} custom-call(f32[16,256,128]{2,1,0:T(8,128)} %ens_ref.1, f32[9,256]{1,0:T(8,128)S(1)} %copy-done.1, f32[256,128]{1,0:T(8,128)S(1)} %copy-done, s32[1,512]{1,0:T(1,128)S(1)} %bitcast.5, s32[1,512]{1,0:T(1,128)S(1)} %bitcast.6, f32[1,512]{1,0:T(1,128)S(1)} %bitcast.7, f32[1,512]{1,0:T(1,128)S(1)} %bitcast.8, ...), custom_call_target="tpu_custom_call" | custom-call | tf_op jit(solution)/shard_map/pallas_call | solution.py:315
  61.5 3.2 %copy.10 = f32[64,64,128]{2,1,0:T(8,128)} copy(f32[64,64,128]{2,1,0:T(8,128)} %shard_map.82) | data formatting | bytes 4194304
Async XLA Ops:
  0.0 0.9 %copy-start = (f32[256,128]{1,0:T(8,128)S(1)}, f32[256,128]{1,0:T(8,128)}, u32[]{:S(2)}) copy-start(f32[256,128]{1,0:T(8,128)} %forc_ref.1) | copy-start | bytes 393220
  0.9 0.7 %copy-start.1 = (f32[9,256]{1,0:T(8,128)S(1)}, f32[9,256]{1,0:T(8,128)}, u32[]{:S(2)}) copy-start(f32[9,256]{1,0:T(8,128)} %sten_ref.1) | copy-start | bytes 27652
  1.6 0.7 %copy-start.2 = (s32[512]{0:T(512)S(1)}, s32[512]{0:T(512)}, u32[]{:S(2)}) copy-start(s32[512]{0:T(512)} %param.11) | copy-start | bytes 6148
  2.3 0.7 %copy-start.3 = (s32[512]{0:T(512)S(1)}, s32[512]{0:T(512)}, u32[]{:S(2)}) copy-start(s32[512]{0:T(512)} %param.12) | copy-start | bytes 6148
  3.0 0.7 %copy-start.4 = (f32[512]{0:T(512)S(1)}, f32[512]{0:T(512)}, u32[]{:S(2)}) copy-start(f32[512]{0:T(512)} %param.13) | copy-start | bytes 6148
  3.7 0.7 %copy-start.5 = (f32[512]{0:T(512)S(1)}, f32[512]{0:T(512)}, u32[]{:S(2)}) copy-start(f32[512]{0:T(512)} %param.14) | copy-start | bytes 6148
  4.4 0.7 %copy-start.6 = (s32[512]{0:T(512)S(1)}, s32[512]{0:T(512)}, u32[]{:S(2)}) copy-start(s32[512]{0:T(512)} %param.15) | copy-start | bytes 6148

commit v3 on v2

--- a/solution.py
+++ b/solution.py
@@ -21,10 +21,9 @@
     q = u * r
     s = 0.5 * u - 5.0 / 3.0
     us = u * s
-    inner = 1.0 + us + (u * q) * (0.625 - 0.25 * u)
-    outer = 4.0 - us + q * (u * (0.625 + u * (1.0 / 12.0)) - 5.0) - (2.0 / 3.0) * r
-    return jnp.where(u <= 1.0, inner, outer)
-
+    near = u <= 1.0
+    cubic = (u * q) * (0.625 + jnp.where(near, -0.25, 1.0 / 12.0) * u)
+    return 1.0 + (cubic + jnp.where(near, us, 3.0 - us - 5.0 * q - (2.0 / 3.0) * r))
 
 def split(value):
     hi = value.astype(jnp.bfloat16)
@@ -210,11 +209,11 @@
 
     def fill_locality(b, low, high):
         lon_sq = lon_part(lon_col[b], lon_here)
-        lat_of = lat_col[b] - first_row
+        lat_of = (lat_col[b] - first_row) * scale_lat
 
         @pl.loop(low, high)
         def _(r):
-            gap = (lat_of - r.astype(f32)) * scale_lat
+            gap = lat_of - r.astype(f32) * scale_lat
             loc[b, r] = locality_of(gap * gap + lon_sq)
 
     early = lat_dev // 2

time: 65 us -> 63.3 us (0.974)
  Pallas kernels: 56.4 us -> 54.8 us
    pallas_call x1, Pallas kernels: 56.4 us -> 54.8 us  [per_device(): pl.pallas_call(functools.partial(kernel, dims), out_shape=jax.ShapeDtypeS...]
where the time goes in v3:
time: 63.3 us; the launch traced here: 63 us
  Pallas kernels  54.8 us (87%)
  local copies, waits for them, and re-layouts  8.19 us (13%)
    pallas_call x1, Pallas kernels, per_device(): pl.pallas_call(functools.partial(kernel, dims), out_shape=jax.ShapeDtypeS...  54.8 us
    unnamed x15, local copies, waits for them, and re-layouts  8.19 us

profile of v3, /device:TPU:0, one launch (start us, length us, event | category | flops | bytes accessed | tf_op | source)
XLA Modules:
  0.0 63.0 jit_solution(7823248511881602884)
XLA Ops:
  0.0 0.0 copy-start
  0.0 0.9 %copy-done = f32[256,128]{1,0:T(8,128)S(1)} copy-done((f32[256,128]{1,0:T(8,128)S(1)}, f32[256,128]{1,0:T(8,128)}, u32[]{:S(2)}) %copy-start) | copy-done | bytes 131096
  0.9 0.0 copy-start.1
  0.9 0.7 %copy-done.1 = f32[9,256]{1,0:T(8,128)S(1)} copy-done((f32[9,256]{1,0:T(8,128)S(1)}, f32[9,256]{1,0:T(8,128)}, u32[]{:S(2)}) %copy-start.1) | copy-done | bytes 9240
  1.6 0.0 copy-start.2
  1.6 0.7 %copy-done.2 = s32[512]{0:T(512)S(1)} copy-done((s32[512]{0:T(512)S(1)}, s32[512]{0:T(512)}, u32[]{:S(2)}) %copy-start.2) | copy-done | bytes 2072
  2.3 0.0 copy-start.3
  2.3 0.7 %copy-done.3 = s32[512]{0:T(512)S(1)} copy-done((s32[512]{0:T(512)S(1)}, s32[512]{0:T(512)}, u32[]{:S(2)}) %copy-start.3) | copy-done | bytes 2072
  3.0 0.0 copy-start.4
  3.0 0.7 %copy-done.4 = f32[512]{0:T(512)S(1)} copy-done((f32[512]{0:T(512)S(1)}, f32[512]{0:T(512)}, u32[]{:S(2)}) %copy-start.4) | copy-done | bytes 2072
  3.7 0.0 copy-start.5
  3.7 0.7 %copy-done.5 = f32[512]{0:T(512)S(1)} copy-done((f32[512]{0:T(512)S(1)}, f32[512]{0:T(512)}, u32[]{:S(2)}) %copy-start.5) | copy-done | bytes 2072
  4.4 0.0 copy-start.6
  4.4 0.7 %copy-done.6 = s32[512]{0:T(512)S(1)} copy-done((s32[512]{0:T(512)S(1)}, s32[512]{0:T(512)}, u32[]{:S(2)}) %copy-start.6) | copy-done | bytes 2072
  5.0 54.8 %shard_map.82 = f32[64,64,128]{2,1,0:T(8,128)} custom-call(f32[16,256,128]{2,1,0:T(8,128)} %ens_ref.1, f32[9,256]{1,0:T(8,128)S(1)} %copy-done.1, f32[256,128]{1,0:T(8,128)S(1)} %copy-done, s32[1,512]{1,0:T(1,128)S(1)} %bitcast.5, s32[1,512]{1,0:T(1,128)S(1)} %bitcast.6, f32[1,512]{1,0:T(1,128)S(1)} %bitcast.7, f32[1,512]{1,0:T(1,128)S(1)} %bitcast.8, ...), custom_call_target="tpu_custom_call" | custom-call | tf_op jit(solution)/shard_map/pallas_call | solution.py:314
  59.8 3.2 %copy.10 = f32[64,64,128]{2,1,0:T(8,128)} copy(f32[64,64,128]{2,1,0:T(8,128)} %shard_map.82) | data formatting | bytes 4194304
Async XLA Ops:
  0.0 0.9 %copy-start = (f32[256,128]{1,0:T(8,128)S(1)}, f32[256,128]{1,0:T(8,128)}, u32[]{:S(2)}) copy-start(f32[256,128]{1,0:T(8,128)} %forc_ref.1) | copy-start | bytes 393220
  0.9 0.7 %copy-start.1 = (f32[9,256]{1,0:T(8,128)S(1)}, f32[9,256]{1,0:T(8,128)}, u32[]{:S(2)}) copy-start(f32[9,256]{1,0:T(8,128)} %sten_ref.1) | copy-start | bytes 27652
  1.6 0.7 %copy-start.2 = (s32[512]{0:T(512)S(1)}, s32[512]{0:T(512)}, u32[]{:S(2)}) copy-start(s32[512]{0:T(512)} %param.11) | copy-start | bytes 6148
  2.3 0.7 %copy-start.3 = (s32[512]{0:T(512)S(1)}, s32[512]{0:T(512)}, u32[]{:S(2)}) copy-start(s32[512]{0:T(512)} %param.12) | copy-start | bytes 6148
  3.0 0.7 %copy-start.4 = (f32[512]{0:T(512)S(1)}, f32[512]{0:T(512)}, u32[]{:S(2)}) copy-start(f32[512]{0:T(512)} %param.13) | copy-start | bytes 6148
  3.7 0.7 %copy-start.5 = (f32[512]{0:T(512)S(1)}, f32[512]{0:T(512)}, u32[]{:S(2)}) copy-start(f32[512]{0:T(512)} %param.14) | copy-start | bytes 6148
  4.4 0.7 %copy-start.6 = (s32[512]{0:T(512)S(1)}, s32[512]{0:T(512)}, u32[]{:S(2)}) copy-start(s32[512]{0:T(512)} %param.15) | copy-start | bytes 6148
